TPU v7x, 256 devices: a whole 4x4x8 slice. The times are simulated.
256 devices in a mesh: rep: 4 (over z_lo), fsdp: 64 (over x, y, z_hi, core).
Axes of the slice: x: 4, y: 4, z: 8 (z_hi: 2, z_lo: 4; z = z_hi * 4 + z_lo), core: 2. Of those that a mesh axis runs over, the one named last changes fastest.
Arguments:
- hidden: bfloat16 [4, 2048, 14336], P('rep', None, 'fsdp'), may hold values from -6 to 6
- out_grad: bfloat16 [4, 2048, 4096], P('rep', None, 'fsdp'), may hold values from -0.52734375 to 0.52734375
- inner_weight: bfloat16 [4, 14336, 4096], P('rep', 'fsdp'), may hold values from -0.59765625 to 0.59765625
- adam_first: bfloat16 [4, 14336, 4096], P('rep', 'fsdp'), may hold values from -6 to 6
- adam_second: bfloat16 [4, 14336, 4096], P('rep', 'fsdp'), may hold values from 0.099609375 to 2
- anchor: float32 [14336, 4096], P('fsdp', 'rep'), may hold values from -0.6 to 0.6
- outer_momentum: float32 [14336, 4096], P('fsdp', 'rep'), may hold values from -0.3 to 0.3
Outputs:
- new_inner: bfloat16 [14336, 4096], P('fsdp')
- new_anchor: float32 [14336, 4096], P('fsdp', 'rep')
- new_momentum: float32 [14336, 4096], P('fsdp', 'rep')
- input_grad: bfloat16 [4, 2048, 14336], P('rep', None, 'fsdp')
All inputs are finite; a program needn't handle non-finite values.
Results may differ from a plain program's by a relative error of at most 0.01.
Values may be sent and summed in bfloat16 or wider, within the bound.
A program may use at most 128 MiB of HBM per device.

v0:
```python
import jax
import jax.numpy as jnp
from jax import lax
from jax.sharding import PartitionSpec as P

BETA_ONE = 0.9
BETA_TWO = 0.95
INNER_RATE = 0.1
DECAY = 0.1
EPSILON = 1e-08
OUTER_RATE = 0.7
OUTER_MU = 0.9


def adamw_step(weight, moment_one, moment_two, weight_grad):
    first = BETA_ONE * moment_one.astype(jnp.float32) + (1.0 - BETA_ONE) * weight_grad
    second = (
        BETA_TWO * moment_two.astype(jnp.float32) + (1.0 - BETA_TWO) * weight_grad * weight_grad
    )
    bias_one = 1.0 - BETA_ONE**10
    bias_two = 1.0 - BETA_TWO**10
    weight_full = weight.astype(jnp.float32)
    update = first / bias_one / (jnp.sqrt(second / bias_two) + EPSILON)
    return (weight_full - INNER_RATE * (update + DECAY * weight_full)).astype(jnp.bfloat16)


def nesterov(anchor_part, moment_part, mean_part):
    delta = anchor_part - mean_part
    moment_next = OUTER_MU * moment_part + delta
    anchor_next = anchor_part - OUTER_RATE * (delta + OUTER_MU * moment_next)
    return (anchor_next, moment_next)


def on_device(hidden, out_grad, inner_weight, adam_first, adam_second, anchor, outer_momentum):
    activations = hidden[0]
    grads_out = out_grad[0]
    weight = inner_weight[0]
    gathered = lax.all_gather(grads_out, "fsdp", axis=1, tiled=True)
    weight_grad = lax.dot_general(
        activations, gathered, (((0,), (0,)), ((), ())), preferred_element_type=jnp.float32
    )
    input_back = lax.dot_general(
        gathered, weight, (((1,), (1,)), ((), ())), preferred_element_type=jnp.float32
    )
    input_grad = input_back.astype(jnp.bfloat16)[None]
    stepped = adamw_step(weight, adam_first[0], adam_second[0], weight_grad)
    replicas = lax.axis_size("rep")
    summed = lax.psum(stepped.astype(jnp.float32), "rep")
    anchor_all, moment_all = (
        lax.all_gather(anchor, "rep", axis=1, tiled=True),
        lax.all_gather(outer_momentum, "rep", axis=1, tiled=True),
    )
    anchor_next_all, moment_next_all = nesterov(anchor_all, moment_all, summed / replicas)
    quarter = anchor.shape[1]
    position = lax.axis_index("rep")
    new_anchor = lax.dynamic_slice_in_dim(anchor_next_all, position * quarter, quarter, 1)
    new_momentum = lax.dynamic_slice_in_dim(moment_next_all, position * quarter, quarter, 1)
    new_inner = anchor_next_all.astype(jnp.bfloat16)
    return (new_inner, new_anchor, new_momentum, input_grad)


def solution(mesh):
    placed = (
        P("rep", None, "fsdp"),
        P("rep", None, "fsdp"),
        P("rep", "fsdp", None),
        P("rep", "fsdp", None),
        P("rep", "fsdp", None),
        P("fsdp", "rep"),
        P("fsdp", "rep"),
    )
    return jax.shard_map(
        on_device,
        mesh=mesh,
        in_specs=placed,
        out_specs=(P("fsdp", None), P("fsdp", "rep"), P("fsdp", "rep"), P("rep", None, "fsdp")),
        check_vma=False,
    )
```

profile of v0, /device:TPU:18, one launch (start us, length us, event | category | flops | bytes accessed | tf_op | source)
XLA Modules:
  0.0 484.9 jit_solution(6842101546593390126)
XLA Ops:
  7.2 0.0 copy-start
  7.2 0.0 all-gather.9.cloned.1.call-start
  7.2 0.7 all-gather.9.cloned.1.call-update
  7.9 0.0 all-gather.5.cloned.1.call-start
  8.0 0.7 all-gather.5.cloned.1.call-update
  8.7 0.0 all-gather.7.cloned.1.call-start
  8.7 0.7 all-gather.7.cloned.1.call-update
  9.4 0.0 all-reduce.2.cloned.1.call-start
  9.4 156.9 %all-gather.9.cloned.1.call-done = bf16[1,2048,4096]{1,2,0:T(8,128)(2,1)} async-done(((bf16[1,2048,64]{1,2,0:T(8,128)(2,1)}), bf16[1,2048,4096]{1,2,0:T(8,128)(2,1)}) %all-gather.9.cloned.1.call-update) | async-done | bytes 16777232 | tf_op jit(solution)/shard_map/all_gather | solution.py:38
  166.4 0.0 copy-done
  166.4 17.4 %fusion.15 = f32[224,4096]{1,0:T(8,128)} fusion(bf16[1,224,4096]{2,1,0:T(8,128)(2,1)} %param.11, bf16[1,2048,4096]{1,2,0:T(8,128)(2,1)} %all-gather.9.cloned.1.call-done, bf16[1,224,4096]{2,1,0:T(8,128)(2,1)} %param.10, bf16[1,224,4096]{2,1,0:T(8,128)(2,1)} %param.9, bf16[1,2048,224]{1,2,0:T(8,128)(2,1)S(1)} %copy-done), kind=kOutput, calls=%fused_computation.20 | convolution fusion | flops 3776446464 | bytes 26869760 | tf_op jit(solution)/shard_map/dot_general | solution.py:39
  183.8 0.0 copy-start.1
  183.8 0.0 all-reduce.2.cloned.1.call-update
  183.8 1.5 copy-done.1
  185.3 9.0 %fusion.21 = bf16[1,2048,224]{1,2,0:T(8,128)(2,1)} fusion(bf16[1,2048,4096]{1,2,0:T(8,128)(2,1)} %all-gather.9.cloned.1.call-done, bf16[1,224,4096]{2,1,0:T(8,128)(2,1)S(1)} %copy-done.1), kind=kOutput, calls=%fused_computation.22 | convolution fusion | flops 3758555136 | bytes 19529728 | tf_op jit(solution)/shard_map/dot_general | solution.py:42
  194.2 47.6 %all-gather.5.cloned.1.call-done = f32[224,4096]{1,0:T(8,128)} async-done(((f32[224,1024]{1,0:T(8,128)}), f32[224,4096]{1,0:T(8,128)}) %all-gather.5.cloned.1.call-update) | async-done | bytes 3670032 | tf_op jit(solution)/shard_map/all_gather | solution.py:50
  241.8 77.4 %all-gather.7.cloned.1.call-done = f32[224,4096]{1,0:T(8,128)} async-done(((f32[224,1024]{1,0:T(8,128)}), f32[224,4096]{1,0:T(8,128)}) %all-gather.7.cloned.1.call-update) | async-done | bytes 3670032 | tf_op jit(solution)/shard_map/all_gather | solution.py:51
  319.2 150.8 %all-reduce.2.cloned.1.call-done = f32[224,4096]{1,0:T(8,128)} async-done(((f32[224,4096]{1,0:T(8,128)}), f32[224,4096]{1,0:T(8,128)}) %all-reduce.2.cloned.1.call-update) | async-done | bytes 3670032 | tf_op jit(solution)/shard_map/psum | solution.py:48
  470.0 6.9 %fusion.26 = (bf16[224,4096]{1,0:T(8,128)(2,1)}, f32[224,4096]{1,0:T(8,128)S(1)}, f32[224,4096]{1,0:T(8,128)S(1)}) fusion(f32[224,4096]{1,0:T(8,128)} %all-gather.5.cloned.1.call-done, f32[224,4096]{1,0:T(8,128)} %all-gather.7.cloned.1.call-done, f32[224,4096]{1,0:T(8,128)} %all-reduce.2.cloned.1.call-done), kind=kLoop, calls=%fused_computation.27 | loop fusion | flops 8257536 | bytes 20185088 | tf_op jit(solution)/shard_map/convert_element_type | solution.py:58
  476.9 1.4 constant_dynamic-slice_fusion
Async XLA Ops:
  7.2 159.2 %copy-start = (bf16[1,2048,224]{1,2,0:T(8,128)(2,1)S(1)}, bf16[1,2048,224]{1,2,0:T(8,128)(2,1)}, u32[]{:S(2)}) copy-start(bf16[1,2048,224]{1,2,0:T(8,128)(2,1)} %param.7) | copy-start | bytes 2752516
  7.2 159.2 %all-gather.9.cloned.1.call-start = ((), (), s32[]{:S(2)}) async-start(), calls=%async_computation.3 | async-start | bytes 17039360 | tf_op jit(solution)/shard_map/all_gather | solution.py:38
  7.9 233.9 %all-gather.5.cloned.1.call-start = ((), (), s32[]{:S(2)}) async-start(), calls=%async_computation | async-start | bytes 4587520 | tf_op jit(solution)/shard_map/all_gather | solution.py:50
  8.7 310.5 %all-gather.7.cloned.1.call-start = ((), (), s32[]{:S(2)}) async-start(), calls=%async_computation.2 | async-start | bytes 4587520 | tf_op jit(solution)/shard_map/all_gather | solution.py:51
  9.4 460.6 %all-reduce.2.cloned.1.call-start = ((), (), s32[]{:S(2)}) async-start(), calls=%async_computation.1 | async-start | bytes 7340032 | tf_op jit(solution)/shard_map/psum | solution.py:48
  183.8 1.5 copy-start.1
Sparse Core Ops, SparseCore 0:
  11.5 154.8 all-gather.8
  168.2 73.5 all-gather.4
  243.6 75.5 all-gather.6
  321.7 148.2 all-reduce.1
where the time goes:
time: 486 us; the launch traced here: 485 us
  waiting for transfers between devices  435 us (90%)
  matrix products  26.4 us (5%)
  between operations  13.8 us (3%)
  other arithmetic  6.9 us (1%)
    all_gather x1, waiting for transfers between devices, on_device(): gathered = lax.all_gather(grads_out, 'fsdp', axis=1, tiled=True)  157 us
    psum x1, waiting for transfers between devices, on_device(): summed = lax.psum(stepped.astype(jnp.float32), 'rep')  151 us
    all_gather x1, waiting for transfers between devices, on_device(): lax.all_gather(outer_momentum, 'rep', axis=1, tiled=True)  77.4 us
    all_gather x1, waiting for transfers between devices, on_device(): lax.all_gather(anchor, 'rep', axis=1, tiled=True)  47.6 us
    dot_general x1, matrix products, on_device(): lax.dot_general(activations, gathered, (((0,), (0,)), ((), ())), preferre...  17.4 us
  transfers between devices with their start and end apart: 4, of which 4 were waited for; matrix products, arithmetic and copies ran while one was open for 5% of the time, Pallas kernels for 0%

commit v1 on v0

v1 whole, which is shorter than its diff:
```python
import functools
import jax
import jax.numpy as jnp
from jax import lax
from jax.experimental import pallas as pl
from jax.experimental.pallas import tpu as pltpu
from jax.sharding import PartitionSpec as P

BETA_ONE = 0.9
BETA_TWO = 0.95
INNER_RATE = 0.1
DECAY = 0.1
EPSILON = 1e-08
OUTER_RATE = 0.7
OUTER_MU = 0.9

MESH = pl.DeviceIdType.MESH
F32 = jnp.float32
BF16 = jnp.bfloat16
UNIT = 128
LAG = 3

EVENTS = (
    (0.0, (0, 0, 0)), (4.9, (3, 0, 0)), (4.9, (1, 0, 0)), (4.9, (0, 3, 0)), (4.9, (0, 1, 0)),
    (10.6, (2, 0, 0)), (10.6, (3, 3, 0)), (10.6, (3, 1, 0)), (13.0, (0, 0, 1)), (13.5, (1, 1, 0)),
    (13.6, (1, 3, 0)), (16.3, (0, 2, 0)), (16.4, (2, 1, 0)), (18.4, (1, 0, 1)), (19.2, (3, 0, 1)),
    (20.0, (0, 1, 1)), (22.0, (2, 3, 0)), (24.1, (2, 0, 1)), (24.8, (0, 3, 1)), (24.9, (3, 2, 0)),
    (24.9, (1, 1, 1)), (27.7, (0, 2, 1)), (30.6, (3, 1, 1)), (33.4, (1, 2, 0)), (36.3, (1, 3, 1)),
    (36.3, (2, 1, 1)), (39.1, (3, 3, 1)), (39.1, (1, 2, 1)), (42.0, (3, 2, 1)), (42.0, (2, 2, 0)),
    (44.8, (2, 3, 1)), (44.8, (2, 2, 1)),
)


def plan():
    when = {key: at for at, key in EVENTS}
    ready = sorted(
        (max(when[a, b, h], when[b, a, h]), h, i) for i, (_, (a, b, h)) in enumerate(EVENTS)
    )
    units, steps, seen = [], [], 0
    for at, _, i in ready:
        units.append(EVENTS[i][1])
        now = []
        while seen < len(EVENTS) and EVENTS[seen][0] <= at:
            now.append(EVENTS[seen][1])
            seen += 1
        steps.append(now)
    return units, steps


UNITS, STEPS = plan()
N_UNITS = len(UNITS)


def packed(values, j):
    words = []
    for first in (0, 16):
        word = 0
        for i, v in enumerate(values[first : first + 16]):
            word |= v << (2 * i)
        words.append(word - (1 << 32) if word >= 1 << 31 else word)
    word = jnp.where(j < 16, jnp.int32(words[0]), jnp.int32(words[1]))
    return lax.shift_right_logical(word, 2 * lax.rem(j, 16)) & 3


def forwards(key):
    a, b, h = key
    out = []
    if key == (0, 0, 0):
        out.append("z")
    if b == 0:
        if a == 0:
            out += ["f+", "f-"]
        elif (a, h) == (3, 0):
            out.append("f+")
        elif (a, h) == (1, 1):
            out.append("f-")
        out += ["s+", "s-"]
    elif (b, h) == (3, 0):
        out.append("s+")
    elif (b, h) == (1, 1):
        out.append("s-")
    return out + ["sib"]


SENDS = {}
for _, _key in EVENTS:
    for _way in forwards(_key):
        SENDS[_key, _way] = len(SENDS)
N_SENDS = len(SENDS)


def kernel(
    h_hbm, g_hbm, w_hbm, m_hbm, v_hbm, anchor_hbm, moment_hbm,
    inner_out, anchor_out, moment_out, back_out,
    grads, acts, weight, first_m, second_m, anchor, moment,
    stepped, from_left, from_right, inner, total, back,
    load_sem, block_recv, sib_recv, block_send,
    sum_send, left_recv, right_recv, part_recv, part_left, part_right, out_sem, last_sem,
):
    rep = lax.axis_index("rep")
    place = lax.axis_index("fsdp")
    core = lax.rem(place, 2)
    zh = lax.rem(lax.div(place, 2), 2)
    y = lax.rem(lax.div(place, 4), 4)
    x = lax.div(place, 16)

    def at(px, py, ph, pc):
        return ((px * 4 + py) * 2 + ph) * 2 + pc

    def moved(a, b):
        dx = a + core * (b - a)
        dy = b + core * (a - b)
        return lax.rem(x + dx, 4), lax.rem(y + dy, 4)

    def chip(a, b):
        return at(*moved(a, b), zh, core)

    ways = {
        "f+": (rep, chip(1, 0)),
        "f-": (rep, chip(3, 0)),
        "s+": (rep, chip(0, 1)),
        "s-": (rep, chip(0, 3)),
        "z": (rep, at(x, y, 1 - zh, core)),
        "sib": (rep, at(x, y, zh, 1 - core)),
    }
    left, right = (rep - 1, place), (rep + 1, place)

    loads = [
        pltpu.make_async_copy(src, dst, load_sem.at[i])
        for i, (src, dst) in enumerate(
            (
                (g_hbm, grads.at[pl.ds(pl.multiple_of(place * 64, 64), 64)]),
                (h_hbm, acts),
                (w_hbm, weight),
                (m_hbm, first_m),
                (v_hbm, second_m),
                (anchor_hbm, anchor),
                (moment_hbm, moment),
            )
        )
    ]
    for load in loads:
        load.start()

    barrier = pltpu.get_barrier_semaphore()
    for way in ways.values():
        pl.semaphore_signal(barrier, inc=1, device_id=way, device_id_type=MESH)

    @pl.when(rep > 0)
    def _():
        pl.semaphore_signal(barrier, inc=1, device_id=left, device_id_type=MESH)

    @pl.when(rep < 3)
    def _():
        pl.semaphore_signal(barrier, inc=1, device_id=right, device_id_type=MESH)

    pl.semaphore_wait(barrier, 6 + (rep > 0).astype(jnp.int32) + (rep < 3).astype(jnp.int32))

    def unit_at(a, b, h):
        px, py = moved(a, b)
        ph = zh + h - 2 * zh * h
        return (px * 4 + py) * 2 + ph

    def block(unit, c):
        return grads.at[pl.ds(pl.multiple_of((unit * 2 + c) * 64, 64), 64)]

    def block_copy(key, way):
        unit = unit_at(*key)
        held = block(unit, core)
        recv = sib_recv if way == "sib" else block_recv
        return pltpu.make_async_remote_copy(
            src_ref=held,
            dst_ref=held,
            send_sem=block_send.at[SENDS[key, way]],
            recv_sem=recv.at[unit],
            device_id=ways[way],
            device_id_type=MESH,
        )

    def arrived(unit, c, sem):
        held = block(unit, c)
        pltpu.make_async_copy(held, held, sem.at[unit]).wait()

    def see_to(key):
        if key == (0, 0, 0):
            loads[0].wait()
        else:
            arrived(unit_at(*key), core, block_recv)
        for way in forwards(key):
            block_copy(key, way).start()

    def sum_copy(j, going_right):
        kept = from_left if going_right else from_right
        recv = left_recv if going_right else right_recv
        return pltpu.make_async_remote_copy(
            src_ref=stepped.at[j],
            dst_ref=kept.at[j],
            send_sem=sum_send.at[j],
            recv_sem=recv.at[j],
            device_id=right if going_right else left,
            device_id_type=MESH,
        )

    def part_copy(j, going_right):
        return pltpu.make_async_remote_copy(
            src_ref=inner.at[j],
            dst_ref=inner.at[j],
            send_sem=(part_right if going_right else part_left).at[j],
            recv_sem=part_recv.at[j],
            device_id=right if going_right else left,
            device_id_type=MESH,
        )

    def wait_on(ref, sem):
        pltpu.make_async_copy(ref, ref, sem).wait()

    def unit_of(j):
        a = packed([u[0] for u in UNITS], j)
        b = packed([u[1] for u in UNITS], j)
        h = packed([u[2] for u in UNITS], j)
        return unit_at(a, b, h), h

    def columns(unit):
        return pl.ds(pl.multiple_of(unit * UNIT, UNIT), UNIT)

    def out_copy(j, unit):
        return pltpu.make_async_copy(inner.at[j], inner_out.at[:, columns(unit)], out_sem.at[j])

    def adamw(j, unit):
        weight_grad = lax.dot_general(
            acts[...],
            grads[columns(unit), :],
            (((1,), (1,)), ((), ())),
            preferred_element_type=F32,
        )
        cols = columns(unit)
        weight_full = weight[:, cols].astype(F32)
        first = BETA_ONE * first_m[:, cols].astype(F32) + (1.0 - BETA_ONE) * weight_grad
        second = (
            BETA_TWO * second_m[:, cols].astype(F32)
            + (1.0 - BETA_TWO) * weight_grad * weight_grad
        )
        bias_one = 1.0 - BETA_ONE**10
        bias_two = 1.0 - BETA_TWO**10
        update = (first * (1.0 / bias_one)) / (jnp.sqrt(second * (1.0 / bias_two)) + EPSILON)
        stepped[j] = (weight_full - INNER_RATE * (update + DECAY * weight_full)).astype(BF16)

    def input_grad(unit):
        rows = pl.ds(pl.multiple_of((unit // 2) * 256, 256), 256)
        for tile in range(4):
            cols = pl.ds(tile * 512, 512)
            total[:, cols] += jnp.dot(
                weight[:, rows], grads[rows, cols], preferred_element_type=F32
            )

    def outer(j, unit, owner):
        cols = pl.ds(pl.multiple_of((unit - owner * 8) * UNIT, UNIT), UNIT)

        @pl.when(owner > 0)
        def _():
            wait_on(from_left.at[j], left_recv.at[j])

        @pl.when(owner < 3)
        def _():
            wait_on(from_right.at[j], right_recv.at[j])

        summed = stepped[j].astype(F32)
        one = jnp.where(owner > 0, from_left[j].astype(F32), 0.0)
        two = jnp.where(owner < 3, from_right[j].astype(F32), 0.0)
        mean = (summed + one + two) * 0.25
        old = anchor[:, cols]
        delta = old - mean
        moment_next = OUTER_MU * moment[:, cols] + delta
        anchor_next = old - OUTER_RATE * (delta + OUTER_MU * moment_next)
        moment[:, cols] = moment_next
        anchor[:, cols] = anchor_next
        inner[j] = anchor_next.astype(BF16)

        @pl.when(owner > 0)
        def _():
            part_copy(j, False).start()

        @pl.when(owner < 3)
        def _():
            part_copy(j, True).start()

        out_copy(j, unit).start()

    def along_rep(t):
        for hop in range(6, 0, -1):
            j = t - hop * LAG

            @pl.when((j >= 0) & (j < N_UNITS))
            def _():
                unit, _h = unit_of(j)
                owner = lax.div(unit, 8)
                last = jnp.maximum(owner, 3 - owner)
                if hop <= 3:

                    @pl.when((rep < owner) & (rep == hop))
                    def _():
                        wait_on(from_left.at[j], left_recv.at[j])
                        stepped[j] = (stepped[j].astype(F32) + from_left[j].astype(F32)).astype(BF16)
                        sum_copy(j, True).start()

                    @pl.when((rep > owner) & (3 - rep == hop))
                    def _():
                        wait_on(from_right.at[j], right_recv.at[j])
                        stepped[j] = (stepped[j].astype(F32) + from_right[j].astype(F32)).astype(BF16)
                        sum_copy(j, False).start()

                if hop in (2, 3):

                    @pl.when((rep == owner) & (last == hop))
                    def _():
                        outer(j, unit, owner)

                if hop >= 3:

                    @pl.when((rep != owner) & (last + jnp.abs(rep - owner) == hop))
                    def _():
                        wait_on(inner.at[j], part_recv.at[j])

                        @pl.when((rep < owner) & (rep > 0))
                        def _():
                            part_copy(j, False).start()

                        @pl.when((rep > owner) & (rep < 3))
                        def _():
                            part_copy(j, True).start()

                        out_copy(j, unit).start()

    def step(t, carry):
        for i, keys in enumerate(STEPS):
            if keys:

                @pl.when(t == i)
                def _():
                    for key in keys:
                        see_to(key)
                    if i == 0:
                        total[...] = jnp.zeros_like(total)
                        for load in loads[1:]:
                            load.wait()

        along_rep(t)

        @pl.when(t < N_UNITS)
        def _():
            unit, h = unit_of(t)
            owner = lax.div(unit, 8)
            arrived(unit, 1 - core, sib_recv)
            adamw(t, unit)

            @pl.when((rep == 0) & (owner > 0))
            def _():
                sum_copy(t, True).start()

            @pl.when((rep == 3) & (owner < 3))
            def _():
                sum_copy(t, False).start()

            @pl.when(h == 1)
            def _():
                input_grad(unit)

            @pl.when(t == N_UNITS - 1)
            def _():
                back[...] = total[...].astype(BF16)
                pltpu.make_async_copy(back, back_out, last_sem.at[0]).start()

        return carry

    lax.fori_loop(0, N_UNITS + 6 * LAG, step, 0)

    pltpu.make_async_copy(anchor, anchor_out, last_sem.at[1]).start()
    pltpu.make_async_copy(moment, moment_out, last_sem.at[2]).start()

    for key, way in SENDS:
        block_copy(key, way).wait_send()

    def finish(j, carry):
        unit, _h = unit_of(j)
        owner = lax.div(unit, 8)

        @pl.when(rep < owner)
        def _():
            sum_copy(j, True).wait_send()

        @pl.when(rep > owner)
        def _():
            sum_copy(j, False).wait_send()

        @pl.when((rep <= owner) & (rep > 0))
        def _():
            part_copy(j, False).wait_send()

        @pl.when((rep >= owner) & (rep < 3))
        def _():
            part_copy(j, True).wait_send()

        out_copy(j, unit).wait()
        return carry

    lax.fori_loop(0, N_UNITS, finish, 0)
    pltpu.make_async_copy(back, back_out, last_sem.at[0]).wait()
    pltpu.make_async_copy(anchor, anchor_out, last_sem.at[1]).wait()
    pltpu.make_async_copy(moment, moment_out, last_sem.at[2]).wait()


def on_device(hidden, out_grad, inner_weight, adam_first, adam_second, anchor, outer_momentum):
    acts = jnp.swapaxes(hidden[0], 0, 1)
    own = jnp.swapaxes(out_grad[0], 0, 1)
    rows, tokens = acts.shape
    width = inner_weight.shape[2]
    quarter = anchor.shape[1]
    anywhere = pl.BlockSpec(memory_space=pl.ANY)
    dma = pltpu.SemaphoreType.DMA
    slots = (N_UNITS, rows, UNIT)
    new_inner, new_anchor, new_momentum, back = pl.pallas_call(
        kernel,
        out_shape=(
            jax.ShapeDtypeStruct((rows, width), BF16),
            jax.ShapeDtypeStruct((rows, quarter), F32),
            jax.ShapeDtypeStruct((rows, quarter), F32),
            jax.ShapeDtypeStruct((rows, tokens), BF16),
        ),
        in_specs=[anywhere] * 7,
        out_specs=(anywhere,) * 4,
        scratch_shapes=[
            pltpu.VMEM((width, tokens), BF16),
            pltpu.VMEM((rows, tokens), BF16),
            pltpu.VMEM((rows, width), BF16),
            pltpu.VMEM((rows, width), BF16),
            pltpu.VMEM((rows, width), BF16),
            pltpu.VMEM((rows, quarter), F32),
            pltpu.VMEM((rows, quarter), F32),
            pltpu.VMEM(slots, BF16),
            pltpu.VMEM(slots, BF16),
            pltpu.VMEM(slots, BF16),
            pltpu.VMEM(slots, BF16),
            pltpu.VMEM((rows, tokens), F32),
            pltpu.VMEM((rows, tokens), BF16),
            dma((7,)),
            dma((N_UNITS,)),
            dma((N_UNITS,)),
            dma((N_SENDS,)),
            dma((N_UNITS,)),
            dma((N_UNITS,)),
            dma((N_UNITS,)),
            dma((N_UNITS,)),
            dma((N_UNITS,)),
            dma((N_UNITS,)),
            dma((N_UNITS,)),
            dma((3,)),
        ],
        compiler_params=pltpu.CompilerParams(
            collective_id=0, has_side_effects=True, vmem_limit_bytes=48 * 2**20
        ),
        cost_estimate=pl.CostEstimate(
            flops=4 * rows * tokens * width,
            bytes_accessed=8 * rows * width + 16 * rows * quarter + 4 * rows * tokens,
            transcendentals=rows * width,
        ),
        name="window_end",
    )(acts, own, inner_weight[0], adam_first[0], adam_second[0], anchor, outer_momentum)
    return (new_inner, new_anchor, new_momentum, jnp.swapaxes(back, 0, 1)[None])


def solution(mesh):
    placed = (
        P("rep", None, "fsdp"),
        P("rep", None, "fsdp"),
        P("rep", "fsdp", None),
        P("rep", "fsdp", None),
        P("rep", "fsdp", None),
        P("fsdp", "rep"),
        P("fsdp", "rep"),
    )
    return jax.shard_map(
        on_device,
        mesh=mesh,
        in_specs=placed,
        out_specs=(P("fsdp", None), P("fsdp", "rep"), P("fsdp", "rep"), P("rep", None, "fsdp")),
        check_vma=False,
    )
```

time: 486 us -> 115 us (0.24)
  the two profiles are of different devices: /device:TPU:18 before, /device:TPU:1 now
where the time goes in v1:
time: 115 us
  Pallas kernels  104 us (90%)
  local copies, waits for them, and re-layouts  10.2 us (9%)
    pallas_call x1, Pallas kernels, on_device(): pl.pallas_call(kernel, out_shape=(jax.ShapeDtypeStruct((rows, width), BF1...  104 us
    unnamed x12, local copies, waits for them, and re-layouts  10.2 us

profile of v1, /device:TPU:1, one launch (start us, length us, event | category | flops | bytes accessed | tf_op | source)
XLA Modules:
  0.0 114.7 jit_solution(4685177208957074536)
XLA Ops:
  0.6 0.0 copy-start
  0.6 1.2 %copy-done = bf16[1,2048,224]{1,2,0:T(8,128)(2,1)S(1)} copy-done((bf16[1,2048,224]{1,2,0:T(8,128)(2,1)S(1)}, bf16[1,2048,224]{1,2,0:T(8,128)(2,1)}, u32[]{:S(2)}) %copy-start) | copy-done | bytes 917528
  1.8 0.0 copy-start.1
  1.8 1.2 %copy-done.1 = f32[224,1024]{1,0:T(8,128)S(1)} copy-done((f32[224,1024]{1,0:T(8,128)S(1)}, f32[224,1024]{1,0:T(8,128)}, u32[]{:S(2)}) %copy-start.1) | copy-done | bytes 917528
  3.0 0.0 copy-start.2
  3.0 1.2 %copy-done.2 = f32[224,1024]{1,0:T(8,128)S(1)} copy-done((f32[224,1024]{1,0:T(8,128)S(1)}, f32[224,1024]{1,0:T(8,128)}, u32[]{:S(2)}) %copy-start.2) | copy-done | bytes 917528
  4.2 0.0 copy-start.3
  4.2 0.9 copy-done.3
  5.1 103.9 %window_end.1 = (bf16[224,4096]{1,0:T(8,128)(2,1)}, f32[224,1024]{1,0:T(8,128)S(1)}, f32[224,1024]{1,0:T(8,128)S(1)}, bf16[224,2048]{1,0:T(8,128)(2,1)S(1)}) custom-call(bf16[224,2048]{1,0:T(8,128)(2,1)S(1)} %bitcast.13, bf16[64,2048]{1,0:T(8,128)(2,1)S(1)} %bitcast.14, bf16[224,4096]{1,0:T(8,128)(2,1)} %bitcast.15, bf16[224,4096]{1,0:T(8,128)(2,1)} %bitcast.16, ...), custom_call_target="tpu_custom_call" | custom-call | flops 7516192768 | bytes 12845056 | tf_op jit(solution)/shard_map/window_end/pallas_call | solution.py:421
  109.0 2.9 %copy.15 = bf16[224,4096]{1,0:T(8,128)(2,1)} copy(bf16[224,4096]{1,0:T(8,128)(2,1)} %get-tuple-element.16) | data formatting | bytes 3670016
  111.9 0.9 copy.16
  112.8 0.9 copy.17
  113.8 0.9 copy.18
Async XLA Ops:
  0.6 1.2 %copy-start = (bf16[1,2048,224]{1,2,0:T(8,128)(2,1)S(1)}, bf16[1,2048,224]{1,2,0:T(8,128)(2,1)}, u32[]{:S(2)}) copy-start(bf16[1,2048,224]{1,2,0:T(8,128)(2,1)} %param.7) | copy-start | bytes 2752516
  1.8 1.2 %copy-start.1 = (f32[224,1024]{1,0:T(8,128)S(1)}, f32[224,1024]{1,0:T(8,128)}, u32[]{:S(2)}) copy-start(f32[224,1024]{1,0:T(8,128)} %anchor_hbm.1) | copy-start | bytes 2752516
  3.0 1.2 %copy-start.2 = (f32[224,1024]{1,0:T(8,128)S(1)}, f32[224,1024]{1,0:T(8,128)}, u32[]{:S(2)}) copy-start(f32[224,1024]{1,0:T(8,128)} %moment_hbm.1) | copy-start | bytes 2752516
  4.2 0.9 copy-start.3

commit v2 on v1

v2 whole, which is shorter than its diff:
```python
import functools
import jax
import jax.numpy as jnp
from jax import lax
from jax.experimental import pallas as pl
from jax.experimental.pallas import tpu as pltpu
from jax.sharding import PartitionSpec as P

BETA_ONE = 0.9
BETA_TWO = 0.95
INNER_RATE = 0.1
DECAY = 0.1
EPSILON = 1e-08
OUTER_RATE = 0.7
OUTER_MU = 0.9

MESH = pl.DeviceIdType.MESH
F32 = jnp.float32
BF16 = jnp.bfloat16
UNIT = 128
LAG = 3

ARRIVALS = (
    (0, 0, 0),
    (3, 0, 0),
    (1, 0, 0),
    (0, 3, 0),
    (0, 1, 0),
    (3, 1, 0),
    (0, 0, 1),
    (2, 0, 0),
    (3, 3, 0),
    (1, 1, 0),
    (3, 0, 1),
    (1, 0, 1),
    (1, 3, 0),
    (0, 1, 1),
    (0, 2, 0),
    (2, 1, 0),
    (0, 3, 1),
    (2, 0, 1),
    (2, 3, 0),
    (3, 1, 1),
    (3, 2, 0),
    (1, 1, 1),
    (3, 3, 1),
    (0, 2, 1),
    (1, 3, 1),
    (2, 1, 1),
    (1, 2, 0),
    (3, 2, 1),
    (2, 3, 1),
    (1, 2, 1),
    (2, 2, 0),
    (2, 2, 1),
)
BEHIND = 4


def plan():
    when = {key: i for i, key in enumerate(ARRIVALS)}
    ready = sorted((max(when[a, b, h], when[b, a, h]), h, when[a, b, h]) for a, b, h in ARRIVALS)
    assert all(at <= i + BEHIND for i, (at, _, _) in enumerate(ready))
    return [ARRIVALS[i] for _, _, i in ready]


UNITS = plan()
N_UNITS = len(UNITS)
REP_HOPS = 6
STEPWISE = 24


def packed(values, j):
    words = []
    for first in (0, 16):
        word = 0
        for i, v in enumerate(values[first : first + 16]):
            word |= v << (2 * i)
        words.append(word - (1 << 32) if word >= 1 << 31 else word)
    word = jnp.where(j < 16, jnp.int32(words[0]), jnp.int32(words[1]))
    return lax.shift_right_logical(word, 2 * lax.rem(j, 16)) & 3


def forwards(key):
    a, b, h = key
    out = []
    if key == (0, 0, 0):
        out.append("z")
    if b == 0:
        if a == 0:
            out += ["f+", "f-"]
        elif (a, h) == (3, 0):
            out.append("f+")
        elif (a, h) == (1, 1):
            out.append("f-")
        out += ["s+", "s-"]
    elif (b, h) == (3, 0):
        out.append("s+")
    elif (b, h) == (1, 1):
        out.append("s-")
    return out + ["sib"]


SENDS = {}
for _key in ARRIVALS:
    for _way in forwards(_key):
        SENDS[_key, _way] = len(SENDS)
N_SENDS = len(SENDS)


def kernel(
    h_hbm, g_hbm, w_hbm, m_hbm, v_hbm, anchor_hbm, moment_hbm,
    inner_out, anchor_out, moment_out, back_out,
    grads, acts, weight, first_m, second_m, anchor, moment,
    stepped, from_near, from_far, inner, total, back,
    load_sem, block_recv, sib_recv, block_send,
    sum_send, near_recv, far_recv, part_recv, part_one, part_two, out_sem, last_sem,
):
    rep = lax.axis_index("rep")
    place = lax.axis_index("fsdp")
    core = lax.rem(place, 2)
    zh = lax.rem(lax.div(place, 2), 2)
    y = lax.rem(lax.div(place, 4), 4)
    x = lax.div(place, 16)

    def at(px, py, ph, pc):
        return ((px * 4 + py) * 2 + ph) * 2 + pc

    def moved(a, b):
        dx = a + core * (b - a)
        dy = b + core * (a - b)
        return lax.rem(x + dx, 4), lax.rem(y + dy, 4)

    def chip(a, b):
        return at(*moved(a, b), zh, core)

    ways = {
        "f+": (rep, chip(1, 0)),
        "f-": (rep, chip(3, 0)),
        "s+": (rep, chip(0, 1)),
        "s-": (rep, chip(0, 3)),
        "z": (rep, at(x, y, 1 - zh, core)),
        "sib": (rep, at(x, y, zh, 1 - core)),
    }

    loads = [
        pltpu.make_async_copy(src, dst, load_sem.at[i])
        for i, (src, dst) in enumerate(
            (
                (g_hbm, grads.at[pl.ds(pl.multiple_of(place * 64, 64), 64)]),
                (h_hbm, acts),
                (w_hbm, weight),
                (m_hbm, first_m),
                (v_hbm, second_m),
                (anchor_hbm, anchor),
                (moment_hbm, moment),
            )
        )
    ]
    for load in loads:
        load.start()

    barrier = pltpu.get_barrier_semaphore()
    for way in ways.values():
        pl.semaphore_signal(barrier, inc=1, device_id=way, device_id_type=MESH)

    for other in range(1, 4):
        pl.semaphore_signal(
            barrier, inc=1, device_id=(lax.rem(rep + other, 4), place), device_id_type=MESH
        )
    pl.semaphore_wait(barrier, 9)

    def unit_at(a, b, h):
        px, py = moved(a, b)
        ph = zh + h - 2 * zh * h
        return (px * 4 + py) * 2 + ph

    def block(unit, c):
        return grads.at[pl.ds(pl.multiple_of((unit * 2 + c) * 64, 64), 64)]

    def block_copy(key, way):
        unit = unit_at(*key)
        held = block(unit, core)
        recv = sib_recv if way == "sib" else block_recv
        return pltpu.make_async_remote_copy(
            src_ref=held,
            dst_ref=held,
            send_sem=block_send.at[SENDS[key, way]],
            recv_sem=recv.at[unit],
            device_id=ways[way],
            device_id_type=MESH,
        )

    def arrived(unit, c, sem):
        held = block(unit, c)
        pltpu.make_async_copy(held, held, sem.at[unit]).wait()

    def see_to(key):
        if key == (0, 0, 0):
            loads[0].wait()
        else:
            arrived(unit_at(*key), core, block_recv)
        for way in forwards(key):
            block_copy(key, way).start()

    def sum_copy(j, target):
        return [
            pltpu.make_async_remote_copy(
                src_ref=stepped.at[j],
                dst_ref=kept.at[j],
                send_sem=sum_send.at[j],
                recv_sem=recv.at[j],
                device_id=(target, place),
                device_id_type=MESH,
            )
            for kept, recv in ((from_near, near_recv), (from_far, far_recv))
        ]

    def part_copy(j, target, sems):
        return pltpu.make_async_remote_copy(
            src_ref=inner.at[j],
            dst_ref=inner.at[j],
            send_sem=sems.at[j],
            recv_sem=part_recv.at[j],
            device_id=(target, place),
            device_id_type=MESH,
        )

    def wait_on(ref, sem):
        pltpu.make_async_copy(ref, ref, sem).wait()

    def unit_of(j):
        a = packed([u[0] for u in UNITS], j)
        b = packed([u[1] for u in UNITS], j)
        h = packed([u[2] for u in UNITS], j)
        return unit_at(a, b, h)

    def columns(unit):
        return pl.ds(pl.multiple_of(unit * UNIT, UNIT), UNIT)

    def out_copy(j, unit):
        return pltpu.make_async_copy(inner.at[j], inner_out.at[:, columns(unit)], out_sem.at[j])

    def adamw(j, unit):
        weight_grad = lax.dot_general(
            acts[...],
            grads[columns(unit), :],
            (((1,), (1,)), ((), ())),
            preferred_element_type=F32,
        )
        cols = columns(unit)
        weight_full = weight[:, cols].astype(F32)
        first = BETA_ONE * first_m[:, cols].astype(F32) + (1.0 - BETA_ONE) * weight_grad
        second = (
            BETA_TWO * second_m[:, cols].astype(F32)
            + (1.0 - BETA_TWO) * weight_grad * weight_grad
        )
        bias_one = 1.0 - BETA_ONE**10
        bias_two = 1.0 - BETA_TWO**10
        update = (first * (1.0 / bias_one)) / (jnp.sqrt(second * (1.0 / bias_two)) + EPSILON)
        stepped[j] = (weight_full - INNER_RATE * (update + DECAY * weight_full)).astype(BF16)

    def input_grad(unit):
        rows = pl.ds(pl.multiple_of((unit // 2) * 256, 256), 256)
        for tile in range(4):
            cols = pl.ds(tile * 512, 512)
            total[:, cols] += jnp.dot(
                weight[:, rows], grads[rows, cols], preferred_element_type=F32
            )

    def roles(owner):
        low = owner < 2
        near = owner + 1 - 2 * lax.rem(owner, 2)
        return near, jnp.where(low, 2, 1), jnp.where(low, 3, 0)

    def outer(j, unit, owner, near, middle, stepwise):
        cols = pl.ds(pl.multiple_of((unit - owner * 8) * UNIT, UNIT), UNIT)
        wait_on(from_near.at[j], near_recv.at[j])

        @pl.when(jnp.logical_not(stepwise))
        def _():
            wait_on(from_far.at[j], far_recv.at[j])

        beyond = jnp.where(stepwise, 0.0, from_far[j].astype(F32))
        summed = stepped[j].astype(F32) + from_near[j].astype(F32) + beyond
        old = anchor[:, cols]
        delta = old - summed * 0.25
        moment_next = OUTER_MU * moment[:, cols] + delta
        anchor_next = old - OUTER_RATE * (delta + OUTER_MU * moment_next)
        inner[j] = anchor_next.astype(BF16)
        part_copy(j, near, part_one).start()

        @pl.when(jnp.logical_not(stepwise))
        def _():
            part_copy(j, middle, part_two).start()

        moment[:, cols] = moment_next
        anchor[:, cols] = anchor_next
        out_copy(j, unit).start()

    def line(j):
        unit = unit_of(j)
        owner = lax.div(unit, 8)
        stepwise = (j < STEPWISE) & ((owner == 0) | (owner == 3))
        return unit, owner, *roles(owner), stepwise

    def first_hop(j):
        _, owner, near, middle, far, stepwise = line(j)

        @pl.when(rep == far)
        def _():
            sum_copy(j, middle)[0].start()

        @pl.when((rep == near) & jnp.logical_not(stepwise))
        def _():
            sum_copy(j, owner)[0].start()

    def add_to(j, kept, recv):
        wait_on(kept.at[j], recv.at[j])
        stepped[j] = (stepped[j].astype(F32) + kept[j].astype(F32)).astype(BF16)

    def take_part(j, unit):
        wait_on(inner.at[j], part_recv.at[j])
        out_copy(j, unit).start()

    def along_rep(t):
        for hop in range(REP_HOPS, 0, -1):
            j = t - hop * LAG

            @pl.when((j >= 0) & (j < (STEPWISE if hop > 4 else N_UNITS)))
            def _():
                unit, owner, near, middle, far, stepwise = line(j)
                direct = jnp.logical_not(stepwise)
                if hop == 1:

                    @pl.when(rep == middle)
                    def _():
                        add_to(j, from_near, near_recv)
                        sum_copy(j, jnp.where(stepwise, near, owner))[1].start()

                if hop == 2:

                    @pl.when((rep == near) & stepwise)
                    def _():
                        add_to(j, from_far, far_recv)
                        sum_copy(j, owner)[0].start()

                if hop in (2, 3):

                    @pl.when((rep == owner) & (stepwise if hop == 3 else direct))
                    def _():
                        outer(j, unit, owner, near, middle, stepwise)

                if hop in (3, 4):

                    @pl.when((rep == near) & (stepwise if hop == 4 else direct))
                    def _():
                        take_part(j, unit)

                        @pl.when(stepwise)
                        def _():
                            part_copy(j, middle, part_one).start()

                if hop in (3, 5):

                    @pl.when((rep == middle) & (stepwise if hop == 5 else direct))
                    def _():
                        take_part(j, unit)
                        part_copy(j, far, part_one).start()

                if hop in (4, 6):

                    @pl.when((rep == far) & (stepwise if hop == 6 else direct))
                    def _():
                        take_part(j, unit)

    def step(t, carry):
        for i, key in enumerate(ARRIVALS):

            @pl.when(t == i)
            def _():
                see_to(key)

        @pl.when(t == 0)
        def _():
            total[...] = jnp.zeros_like(total)

        @pl.when(t == BEHIND)
        def _():
            for load in loads[1:]:
                load.wait()

        j = t - BEHIND
        along_rep(j)

        @pl.when((j >= 0) & (j < N_UNITS))
        def _():
            unit = unit_of(j)
            arrived(unit, 1 - core, sib_recv)
            adamw(j, unit)
            first_hop(j)

        for half in range(2):
            position = 2 * (j - N_UNITS) + half

            @pl.when((position >= 0) & (position < 16))
            def _():
                input_grad(2 * position)

        @pl.when(j == N_UNITS + 7)
        def _():
            back[...] = total[...].astype(BF16)
            pltpu.make_async_copy(back, back_out, last_sem.at[0]).start()

        return carry

    lax.fori_loop(0, BEHIND + N_UNITS + max(4 * LAG, STEPWISE - N_UNITS + 6 * LAG, 8), step, 0)

    pltpu.make_async_copy(anchor, anchor_out, last_sem.at[1]).start()
    pltpu.make_async_copy(moment, moment_out, last_sem.at[2]).start()

    for key, way in SENDS:
        block_copy(key, way).wait_send()

    def finish(j, carry):
        unit, owner, near, middle, far, stepwise = line(j)

        @pl.when(rep != owner)
        def _():
            sum_copy(j, owner)[0].wait_send()

        @pl.when((rep == owner) | (rep == middle) | ((rep == near) & stepwise))
        def _():
            part_copy(j, near, part_one).wait_send()

        @pl.when((rep == owner) & jnp.logical_not(stepwise))
        def _():
            part_copy(j, near, part_two).wait_send()

        out_copy(j, unit).wait()
        return carry

    lax.fori_loop(0, N_UNITS, finish, 0)
    pltpu.make_async_copy(back, back_out, last_sem.at[0]).wait()
    pltpu.make_async_copy(anchor, anchor_out, last_sem.at[1]).wait()
    pltpu.make_async_copy(moment, moment_out, last_sem.at[2]).wait()


def write_out(*refs):
    sems = refs[8]
    copies = [pltpu.make_async_copy(refs[i], refs[4 + i], sems.at[i]) for i in range(4)]
    for copy in copies:
        copy.start()
    for copy in copies:
        copy.wait()


def on_device(hidden, out_grad, inner_weight, adam_first, adam_second, anchor, outer_momentum):
    acts = jnp.swapaxes(hidden[0], 0, 1)
    own = jnp.swapaxes(out_grad[0], 0, 1)
    rows, tokens = acts.shape
    width = inner_weight.shape[2]
    quarter = anchor.shape[1]
    anywhere = pl.BlockSpec(memory_space=pl.ANY)
    dma = pltpu.SemaphoreType.DMA
    slots = (N_UNITS, rows, UNIT)
    results = pl.pallas_call(
        kernel,
        out_shape=(
            jax.ShapeDtypeStruct((rows, width), BF16),
            jax.ShapeDtypeStruct((rows, quarter), F32),
            jax.ShapeDtypeStruct((rows, quarter), F32),
            jax.ShapeDtypeStruct((rows, tokens), BF16),
        ),
        in_specs=[anywhere] * 7,
        out_specs=(anywhere,) * 4,
        scratch_shapes=[
            pltpu.VMEM((width, tokens), BF16),
            pltpu.VMEM((rows, tokens), BF16),
            pltpu.VMEM((rows, width), BF16),
            pltpu.VMEM((rows, width), BF16),
            pltpu.VMEM((rows, width), BF16),
            pltpu.VMEM((rows, quarter), F32),
            pltpu.VMEM((rows, quarter), F32),
            pltpu.VMEM(slots, BF16),
            pltpu.VMEM(slots, BF16),
            pltpu.VMEM(slots, BF16),
            pltpu.VMEM(slots, BF16),
            pltpu.VMEM((rows, tokens), F32),
            pltpu.VMEM((rows, tokens), BF16),
            dma((7,)),
            dma((N_UNITS,)),
            dma((N_UNITS,)),
            dma((N_SENDS,)),
            dma((N_UNITS,)),
            dma((N_UNITS,)),
            dma((N_UNITS,)),
            dma((N_UNITS,)),
            dma((N_UNITS,)),
            dma((N_UNITS,)),
            dma((N_UNITS,)),
            dma((3,)),
        ],
        compiler_params=pltpu.CompilerParams(
            collective_id=0, has_side_effects=True, vmem_limit_bytes=48 * 2**20
        ),
        cost_estimate=pl.CostEstimate(
            flops=4 * rows * tokens * width,
            bytes_accessed=8 * rows * width + 16 * rows * quarter + 4 * rows * tokens,
            transcendentals=rows * width,
        ),
        name="window_end",
    )(
        *(
            pltpu.with_memory_space_constraint(a, pltpu.HBM)
            for a in (acts, own, inner_weight[0], adam_first[0], adam_second[0], anchor, outer_momentum)
        )
    )
    new_inner, new_anchor, new_momentum, back = pl.pallas_call(
        write_out,
        out_shape=tuple(jax.ShapeDtypeStruct(r.shape, r.dtype) for r in results),
        in_specs=[anywhere] * 4,
        out_specs=(anywhere,) * 4,
        scratch_shapes=[dma((4,))],
        compiler_params=pltpu.CompilerParams(vmem_limit_bytes=2**20),
        name="write_out",
    )(*results)
    return (new_inner, new_anchor, new_momentum, jnp.swapaxes(back, 0, 1)[None])


def solution(mesh):
    placed = (
        P("rep", None, "fsdp"),
        P("rep", None, "fsdp"),
        P("rep", "fsdp", None),
        P("rep", "fsdp", None),
        P("rep", "fsdp", None),
        P("fsdp", "rep"),
        P("fsdp", "rep"),
    )
    return jax.shard_map(
        on_device,
        mesh=mesh,
        in_specs=placed,
        out_specs=(P("fsdp", None), P("fsdp", "rep"), P("fsdp", "rep"), P("rep", None, "fsdp")),
        check_vma=False,
    )
```

time: 115 us -> 103 us (0.90)
  the two profiles are of different devices: /device:TPU:1 before, /device:TPU:18 now
where the time goes in v2:
time: 103 us; the launch traced here: 102 us
  Pallas kernels  102 us (99%)
    pallas_call x1, Pallas kernels, on_device(): pl.pallas_call(kernel, out_shape=(jax.ShapeDtypeStruct((rows, width), BF1...  99.5 us
    pallas_call x1, Pallas kernels, on_device(): pl.pallas_call(write_out, out_shape=tuple((jax.ShapeDtypeStruct(r.shape,...  2.17 us

profile of v2, /device:TPU:18, one launch (start us, length us, event | category | flops | bytes accessed | tf_op | source)
XLA Modules:
  0.0 102.3 jit_solution(15172320508140042991)
XLA Ops:
  0.6 99.5 %window_end.1 = (bf16[224,4096]{1,0:T(8,128)(2,1)S(1)}, f32[224,1024]{1,0:T(8,128)S(1)}, f32[224,1024]{1,0:T(8,128)S(1)}, bf16[224,2048]{1,0:T(8,128)(2,1)S(1)}) custom-call(bf16[224,2048]{1,0:T(8,128)(2,1)} %bitcast.15, bf16[64,2048]{1,0:T(8,128)(2,1)} %bitcast.17, bf16[224,4096]{1,0:T(8,128)(2,1)} %bitcast.12, bf16[224,4096]{1,0:T(8,128)(2,1)} %bitcast.13, ...), custom_call_target="tpu_custom_call" | custom-call | flops 7516192768 | bytes 12845056 | tf_op jit(solution)/shard_map/window_end/pallas_call | solution.py:467
  100.1 2.2 %write_out.1 = (bf16[224,4096]{1,0:T(8,128)(2,1)}, f32[224,1024]{1,0:T(8,128)}, f32[224,1024]{1,0:T(8,128)}, bf16[224,2048]{1,0:T(8,128)(2,1)}) custom-call(bf16[224,4096]{1,0:T(8,128)(2,1)S(1)} %get-tuple-element.12.refs_0_, f32[224,1024]{1,0:T(8,128)S(1)} %get-tuple-element.13.refs_1_, f32[224,1024]{1,0:T(8,128)S(1)} %get-tuple-element.14.refs_2_, ...), custom_call_target="tpu_custom_call" | custom-call | tf_op jit(solution)/shard_map/write_out/pallas_call | solution.py:519

commit v3 on v2

--- a/solution.py
+++ b/solution.py
@@ -31,30 +31,30 @@
     (2, 0, 0),
     (3, 3, 0),
     (1, 1, 0),
-    (3, 0, 1),
-    (1, 0, 1),
     (1, 3, 0),
     (0, 1, 1),
+    (1, 0, 1),
     (0, 2, 0),
     (2, 1, 0),
+    (3, 0, 1),
     (0, 3, 1),
+    (2, 3, 0),
     (2, 0, 1),
-    (2, 3, 0),
+    (0, 2, 1),
+    (3, 2, 0),
     (3, 1, 1),
-    (3, 2, 0),
+    (1, 2, 0),
     (1, 1, 1),
+    (1, 3, 1),
     (3, 3, 1),
-    (0, 2, 1),
-    (1, 3, 1),
+    (3, 2, 1),
+    (2, 2, 0),
+    (2, 3, 1),
     (2, 1, 1),
-    (1, 2, 0),
-    (3, 2, 1),
-    (2, 3, 1),
     (1, 2, 1),
-    (2, 2, 0),
     (2, 2, 1),
 )
-BEHIND = 4
+BEHIND = 3
 
 
 def plan():
@@ -67,7 +67,10 @@
 UNITS = plan()
 N_UNITS = len(UNITS)
 REP_HOPS = 6
-STEPWISE = 24
+STEPWISE = 26
+
+TAIL = max(4 * LAG, STEPWISE - N_UNITS + 6 * LAG, 8)
+EARLY = min(2 * TAIL, 2 * (N_UNITS - 6 * LAG) - 2)
 
 
 def packed(values, j):
@@ -270,7 +273,7 @@
 
     def roles(owner):
         low = owner < 2
-        near = owner + 1 - 2 * lax.rem(owner, 2)
+        near = owner ^ 1
         return near, jnp.where(low, 2, 1), jnp.where(low, 3, 0)
 
     def outer(j, unit, owner, near, middle, stepwise):
@@ -298,14 +301,13 @@
         anchor[:, cols] = anchor_next
         out_copy(j, unit).start()
 
-    def line(j):
-        unit = unit_of(j)
-        owner = lax.div(unit, 8)
+    def line(j, unit):
+        owner = unit >> 3
         stepwise = (j < STEPWISE) & ((owner == 0) | (owner == 3))
-        return unit, owner, *roles(owner), stepwise
-
-    def first_hop(j):
-        _, owner, near, middle, far, stepwise = line(j)
+        return owner, *roles(owner), stepwise
+
+    def first_hop(j, unit):
+        owner, near, middle, far, stepwise = line(j, unit)
 
         @pl.when(rep == far)
         def _():
@@ -323,13 +325,14 @@
         wait_on(inner.at[j], part_recv.at[j])
         out_copy(j, unit).start()
 
-    def along_rep(t):
+    def along_rep(t, units):
         for hop in range(REP_HOPS, 0, -1):
             j = t - hop * LAG
 
             @pl.when((j >= 0) & (j < (STEPWISE if hop > 4 else N_UNITS)))
             def _():
-                unit, owner, near, middle, far, stepwise = line(j)
+                unit = units[hop * LAG - 1]
+                owner, near, middle, far, stepwise = line(j, unit)
                 direct = jnp.logical_not(stepwise)
                 if hop == 1:
 
@@ -374,7 +377,7 @@
                     def _():
                         take_part(j, unit)
 
-    def step(t, carry):
+    def step(t, units):
         for i, key in enumerate(ARRIVALS):
 
             @pl.when(t == i)
@@ -391,14 +394,14 @@
                 load.wait()
 
         j = t - BEHIND
-        along_rep(j)
+        along_rep(j, units)
+        unit = unit_of(jnp.minimum(jnp.maximum(j, 0), N_UNITS - 1))
 
         @pl.when((j >= 0) & (j < N_UNITS))
         def _():
-            unit = unit_of(j)
             arrived(unit, 1 - core, sib_recv)
             adamw(j, unit)
-            first_hop(j)
+            first_hop(j, unit)
 
         for half in range(2):
             position = 2 * (j - N_UNITS) + half
@@ -412,18 +415,28 @@
             back[...] = total[...].astype(BF16)
             pltpu.make_async_copy(back, back_out, last_sem.at[0]).start()
 
-        return carry
-
-    lax.fori_loop(0, BEHIND + N_UNITS + max(4 * LAG, STEPWISE - N_UNITS + 6 * LAG, 8), step, 0)
-
-    pltpu.make_async_copy(anchor, anchor_out, last_sem.at[1]).start()
-    pltpu.make_async_copy(moment, moment_out, last_sem.at[2]).start()
-
-    for key, way in SENDS:
-        block_copy(key, way).wait_send()
+        @pl.when(j == N_UNITS + 3 * LAG - 1)
+        def _():
+            pltpu.make_async_copy(anchor, anchor_out, last_sem.at[1]).start()
+            pltpu.make_async_copy(moment, moment_out, last_sem.at[2]).start()
+
+        @pl.when(j == N_UNITS + 2 * LAG)
+        def _():
+            for key, way in SENDS:
+                block_copy(key, way).wait_send()
+
+        for half in range(2):
+            old = 2 * (j - N_UNITS) + half
+
+            @pl.when((old >= 0) & (old < EARLY))
+            def _():
+                finish(old, 0)
+
+        return (unit, *units[:-1])
 
     def finish(j, carry):
-        unit, owner, near, middle, far, stepwise = line(j)
+        unit = unit_of(j)
+        owner, near, middle, far, stepwise = line(j, unit)
 
         @pl.when(rep != owner)
         def _():
@@ -440,7 +453,8 @@
         out_copy(j, unit).wait()
         return carry
 
-    lax.fori_loop(0, N_UNITS, finish, 0)
+    lax.fori_loop(0, BEHIND + N_UNITS + TAIL, step, (jnp.int32(0),) * (6 * LAG))
+    lax.fori_loop(EARLY, N_UNITS, finish, 0)
     pltpu.make_async_copy(back, back_out, last_sem.at[0]).wait()
     pltpu.make_async_copy(anchor, anchor_out, last_sem.at[1]).wait()
     pltpu.make_async_copy(moment, moment_out, last_sem.at[2]).wait()
@@ -448,7 +462,13 @@
 
 def write_out(*refs):
     sems = refs[8]
-    copies = [pltpu.make_async_copy(refs[i], refs[4 + i], sems.at[i]) for i in range(4)]
+    copies = []
+    for i in range(4):
+        half = refs[i].shape[0] // 2
+        for rows in (pl.ds(0, half), pl.ds(half, half)):
+            copies.append(
+                pltpu.make_async_copy(refs[i].at[rows], refs[4 + i].at[rows], sems.at[len(copies)])
+            )
     for copy in copies:
         copy.start()
     for copy in copies:
@@ -521,7 +541,7 @@
         out_shape=tuple(jax.ShapeDtypeStruct(r.shape, r.dtype) for r in results),
         in_specs=[anywhere] * 4,
         out_specs=(anywhere,) * 4,
-        scratch_shapes=[dma((4,))],
+        scratch_shapes=[dma((8,))],
         compiler_params=pltpu.CompilerParams(vmem_limit_bytes=2**20),
         name="write_out",
     )(*results)

time: 103 us -> 96.8 us (0.940)
  Pallas kernels: 102 us -> 96.1 us
    pallas_call x1, Pallas kernels: 99.5 us -> 93.9 us  [on_device(): pl.pallas_call(kernel, out_shape=(jax.ShapeDtypeStruct((rows, width), BF1...]
where the time goes in v3:
time: 96.8 us; the launch traced here: 96.7 us
  Pallas kernels  96.1 us (99%)
    pallas_call x1, Pallas kernels, on_device(): pl.pallas_call(kernel, out_shape=(jax.ShapeDtypeStruct((rows, width), BF1...  93.9 us
    pallas_call x1, Pallas kernels, on_device(): pl.pallas_call(write_out, out_shape=tuple((jax.ShapeDtypeStruct(r.shape,...  2.2 us

profile of v3, /device:TPU:18, one launch (start us, length us, event | category | flops | bytes accessed | tf_op | source)
XLA Modules:
  0.0 96.7 jit_solution(6365803491569173425)
XLA Ops:
  0.6 93.9 %window_end.1 = (bf16[224,4096]{1,0:T(8,128)(2,1)S(1)}, f32[224,1024]{1,0:T(8,128)S(1)}, f32[224,1024]{1,0:T(8,128)S(1)}, bf16[224,2048]{1,0:T(8,128)(2,1)S(1)}) custom-call(bf16[224,2048]{1,0:T(8,128)(2,1)} %bitcast.15, bf16[64,2048]{1,0:T(8,128)(2,1)} %bitcast.17, bf16[224,4096]{1,0:T(8,128)(2,1)} %bitcast.12, bf16[224,4096]{1,0:T(8,128)(2,1)} %bitcast.13, ...), custom_call_target="tpu_custom_call" | custom-call | flops 7516192768 | bytes 12845056 | tf_op jit(solution)/shard_map/window_end/pallas_call | solution.py:487
  94.5 2.2 %write_out.1 = (bf16[224,4096]{1,0:T(8,128)(2,1)}, f32[224,1024]{1,0:T(8,128)}, f32[224,1024]{1,0:T(8,128)}, bf16[224,2048]{1,0:T(8,128)(2,1)}) custom-call(bf16[224,4096]{1,0:T(8,128)(2,1)S(1)} %get-tuple-element.12.refs_0_, f32[224,1024]{1,0:T(8,128)S(1)} %get-tuple-element.13.refs_1_, f32[224,1024]{1,0:T(8,128)S(1)} %get-tuple-element.14.refs_2_, ...), custom_call_target="tpu_custom_call" | custom-call | tf_op jit(solution)/shard_map/write_out/pallas_call | solution.py:539

commit v4 on v3

--- a/solution.py
+++ b/solution.py
@@ -18,7 +18,7 @@
 F32 = jnp.float32
 BF16 = jnp.bfloat16
 UNIT = 128
-LAG = 3
+HOPS = (3, 6, 9, 12, 15, 18)
 
 ARRIVALS = (
     (0, 0, 0),
@@ -66,11 +66,10 @@
 
 UNITS = plan()
 N_UNITS = len(UNITS)
-REP_HOPS = 6
-STEPWISE = 26
-
-TAIL = max(4 * LAG, STEPWISE - N_UNITS + 6 * LAG, 8)
-EARLY = min(2 * TAIL, 2 * (N_UNITS - 6 * LAG) - 2)
+STEPWISE = 25
+
+TAIL = max(HOPS[3], STEPWISE - N_UNITS + HOPS[5], 8)
+EARLY = min(2 * TAIL, 2 * (N_UNITS - HOPS[5]) - 2)
 
 
 def packed(values, j):
@@ -160,9 +159,6 @@
             )
         )
     ]
-    for load in loads:
-        load.start()
-
     barrier = pltpu.get_barrier_semaphore()
     for way in ways.values():
         pl.semaphore_signal(barrier, inc=1, device_id=way, device_id_type=MESH)
@@ -171,6 +167,9 @@
         pl.semaphore_signal(
             barrier, inc=1, device_id=(lax.rem(rep + other, 4), place), device_id_type=MESH
         )
+    for load in loads:
+        load.start()
+
     pl.semaphore_wait(barrier, 9)
 
     def unit_at(a, b, h):
@@ -326,12 +325,12 @@
         out_copy(j, unit).start()
 
     def along_rep(t, units):
-        for hop in range(REP_HOPS, 0, -1):
-            j = t - hop * LAG
+        for hop in range(6, 0, -1):
+            j = t - HOPS[hop - 1]
 
             @pl.when((j >= 0) & (j < (STEPWISE if hop > 4 else N_UNITS)))
             def _():
-                unit = units[hop * LAG - 1]
+                unit = units[HOPS[hop - 1] - 1]
                 owner, near, middle, far, stepwise = line(j, unit)
                 direct = jnp.logical_not(stepwise)
                 if hop == 1:
@@ -415,12 +414,12 @@
             back[...] = total[...].astype(BF16)
             pltpu.make_async_copy(back, back_out, last_sem.at[0]).start()
 
-        @pl.when(j == N_UNITS + 3 * LAG - 1)
+        @pl.when(j == N_UNITS + HOPS[2] - 1)
         def _():
             pltpu.make_async_copy(anchor, anchor_out, last_sem.at[1]).start()
             pltpu.make_async_copy(moment, moment_out, last_sem.at[2]).start()
 
-        @pl.when(j == N_UNITS + 2 * LAG)
+        @pl.when(j == N_UNITS + HOPS[1])
         def _():
             for key, way in SENDS:
                 block_copy(key, way).wait_send()
@@ -453,7 +452,7 @@
         out_copy(j, unit).wait()
         return carry
 
-    lax.fori_loop(0, BEHIND + N_UNITS + TAIL, step, (jnp.int32(0),) * (6 * LAG))
+    lax.fori_loop(0, BEHIND + N_UNITS + TAIL, step, (jnp.int32(0),) * HOPS[5])
     lax.fori_loop(EARLY, N_UNITS, finish, 0)
     pltpu.make_async_copy(back, back_out, last_sem.at[0]).wait()
     pltpu.make_async_copy(anchor, anchor_out, last_sem.at[1]).wait()

time: 96.8 us -> 96.5 us (level)
  no operation moved by 1% of the time
where the time goes in v4:
time: 96.5 us; the launch traced here: 96.4 us
  Pallas kernels  95.8 us (99%)
    pallas_call x1, Pallas kernels, on_device(): pl.pallas_call(kernel, out_shape=(jax.ShapeDtypeStruct((rows, width), BF1...  93.6 us
    pallas_call x1, Pallas kernels, on_device(): pl.pallas_call(write_out, out_shape=tuple((jax.ShapeDtypeStruct(r.shape,...  2.2 us

profile of v4, /device:TPU:18, one launch (start us, length us, event | category | flops | bytes accessed | tf_op | source)
XLA Modules:
  0.0 96.4 jit_solution(949793950910728309)
XLA Ops:
  0.6 93.6 %window_end.1 = (bf16[224,4096]{1,0:T(8,128)(2,1)S(1)}, f32[224,1024]{1,0:T(8,128)S(1)}, f32[224,1024]{1,0:T(8,128)S(1)}, bf16[224,2048]{1,0:T(8,128)(2,1)S(1)}) custom-call(bf16[224,2048]{1,0:T(8,128)(2,1)} %bitcast.15, bf16[64,2048]{1,0:T(8,128)(2,1)} %bitcast.17, bf16[224,4096]{1,0:T(8,128)(2,1)} %bitcast.12, bf16[224,4096]{1,0:T(8,128)(2,1)} %bitcast.13, ...), custom_call_target="tpu_custom_call" | custom-call | flops 7516192768 | bytes 12845056 | tf_op jit(solution)/shard_map/window_end/pallas_call | solution.py:486
  94.2 2.2 %write_out.1 = (bf16[224,4096]{1,0:T(8,128)(2,1)}, f32[224,1024]{1,0:T(8,128)}, f32[224,1024]{1,0:T(8,128)}, bf16[224,2048]{1,0:T(8,128)(2,1)}) custom-call(bf16[224,4096]{1,0:T(8,128)(2,1)S(1)} %get-tuple-element.12.refs_0_, f32[224,1024]{1,0:T(8,128)S(1)} %get-tuple-element.13.refs_1_, f32[224,1024]{1,0:T(8,128)S(1)} %get-tuple-element.14.refs_2_, ...), custom_call_target="tpu_custom_call" | custom-call | tf_op jit(solution)/shard_map/write_out/pallas_call | solution.py:538

commit v5 on v4

--- a/solution.py
+++ b/solution.py
@@ -54,6 +54,7 @@
     (1, 2, 1),
     (2, 2, 1),
 )
+LATER = 4
 BEHIND = 3
 
 
@@ -402,14 +403,14 @@
             adamw(j, unit)
             first_hop(j, unit)
 
-        for half in range(2):
-            position = 2 * (j - N_UNITS) + half
-
-            @pl.when((position >= 0) & (position < 16))
-            def _():
-                input_grad(2 * position)
-
-        @pl.when(j == N_UNITS + 7)
+        done = j - LATER
+        second = packed([u[2] for u in UNITS], jnp.minimum(jnp.maximum(done, 0), N_UNITS - 1))
+
+        @pl.when((done >= 0) & (done < N_UNITS) & (second == 1))
+        def _():
+            input_grad(units[LATER - 1])
+
+        @pl.when(j == N_UNITS + LATER)
         def _():
             back[...] = total[...].astype(BF16)
             pltpu.make_async_copy(back, back_out, last_sem.at[0]).start()

time: 96.5 us -> 96.8 us (level)
  no operation moved by 1% of the time
where the time goes in v5:
time: 96.8 us; the launch traced here: 96.7 us
  Pallas kernels  96.1 us (99%)
    pallas_call x1, Pallas kernels, on_device(): pl.pallas_call(kernel, out_shape=(jax.ShapeDtypeStruct((rows, width), BF1...  93.9 us
    pallas_call x1, Pallas kernels, on_device(): pl.pallas_call(write_out, out_shape=tuple((jax.ShapeDtypeStruct(r.shape,...  2.2 us

profile of v5, /device:TPU:18, one launch (start us, length us, event | category | flops | bytes accessed | tf_op | source)
XLA Modules:
  0.0 96.7 jit_solution(13416171764207999590)
XLA Ops:
  0.6 93.9 %window_end.1 = (bf16[224,4096]{1,0:T(8,128)(2,1)S(1)}, f32[224,1024]{1,0:T(8,128)S(1)}, f32[224,1024]{1,0:T(8,128)S(1)}, bf16[224,2048]{1,0:T(8,128)(2,1)S(1)}) custom-call(bf16[224,2048]{1,0:T(8,128)(2,1)} %bitcast.15, bf16[64,2048]{1,0:T(8,128)(2,1)} %bitcast.17, bf16[224,4096]{1,0:T(8,128)(2,1)} %bitcast.12, bf16[224,4096]{1,0:T(8,128)(2,1)} %bitcast.13, ...), custom_call_target="tpu_custom_call" | custom-call | flops 7516192768 | bytes 12845056 | tf_op jit(solution)/shard_map/window_end/pallas_call | solution.py:487
  94.5 2.2 %write_out.1 = (bf16[224,4096]{1,0:T(8,128)(2,1)}, f32[224,1024]{1,0:T(8,128)}, f32[224,1024]{1,0:T(8,128)}, bf16[224,2048]{1,0:T(8,128)(2,1)}) custom-call(bf16[224,4096]{1,0:T(8,128)(2,1)S(1)} %get-tuple-element.12.refs_0_, f32[224,1024]{1,0:T(8,128)S(1)} %get-tuple-element.13.refs_1_, f32[224,1024]{1,0:T(8,128)S(1)} %get-tuple-element.14.refs_2_, ...), custom_call_target="tpu_custom_call" | custom-call | tf_op jit(solution)/shard_map/write_out/pallas_call | solution.py:539
